TPU v7x, 32 devices: a whole 2x2x4 slice. The times are simulated.
32 devices in a mesh: stn: 4 (over x, core), tm: 8 (over z, y).
Axes of the slice: x: 2, y: 2, z: 4, core: 2. Of those that a mesh axis runs over, the one named last changes fastest.
Arguments:
- samples: bfloat16 [2, 1024, 8, 20736], P(None, 'stn', 'tm'), may hold values from -22 to 22
- filter_taps: float32 [6, 3456], replicated, may hold values from -2.5 to 2.5
- station_flags: int32 [1024], P('stn'), may hold values 0 or 1
- channel_keep: int32 [3456], replicated, may hold values from 0 to 1, as said below
- beam_delay: int32 [64, 1024], replicated, may hold values from 0 to 3455
Outputs:
- visibilities: float32 [16, 2, 1024, 1024], P(None, None, 'stn', 'tm')
- beam_power: float32 [64, 3456], P('stn', 'tm')
Inputs may be any that keep to these rules, and one draw needn't show every extreme that they name: `channel_keep`: each value is 0 or 1, and the first fine channel of every output channel is 1.
All inputs are finite; a program needn't handle non-finite values. No bound on the sum of `station_flags` on one device may be relied on, other than what follows from the above.
Results may differ from a plain program's by a relative error of at most 0.013.
Values may be sent and summed in bfloat16 or wider, within the bound.
A program may use at most 128 MiB of HBM per device.

v0:
```python
import math
import jax
import jax.numpy as jnp
from jax import lax
from jax.sharding import PartitionSpec as P

INPUTS = 1024
FINE = 3456
OUTCH = 16
TAPS = 6
TRANSFORM_PRECISION = lax.Precision.HIGH


def phase_table(row_count, col_count, modulus):
    row_ids = lax.broadcasted_iota(jnp.int32, (row_count, col_count), 0)
    col_ids = lax.broadcasted_iota(jnp.int32, (row_count, col_count), 1)
    angles = (row_ids * col_ids % modulus).astype(jnp.float32) * (2.0 * math.pi / modulus)
    return (jnp.cos(angles), jnp.sin(angles))


def fine_spectra(samples, filter_taps, station_flags):
    inputs_dev = samples.shape[1]
    spec_dev = samples.shape[2]
    framed = samples.reshape(2, inputs_dev, spec_dev, TAPS, FINE)
    branch = jnp.sum(framed.astype(jnp.float32) * filter_taps[None, None, None], axis=3)
    fft_inner = 128
    fft_outer = FINE // fft_inner
    grid_view = branch.reshape(2, inputs_dev, spec_dev, fft_outer, fft_inner)
    cos_outer, sin_outer = phase_table(fft_outer, fft_outer, fft_outer)
    first_real = jnp.einsum(
        "kn,isnm->iskm", cos_outer, grid_view[0], precision=TRANSFORM_PRECISION
    ) + jnp.einsum("kn,isnm->iskm", sin_outer, grid_view[1], precision=TRANSFORM_PRECISION)
    first_imag = jnp.einsum(
        "kn,isnm->iskm", cos_outer, grid_view[1], precision=TRANSFORM_PRECISION
    ) - jnp.einsum("kn,isnm->iskm", sin_outer, grid_view[0], precision=TRANSFORM_PRECISION)
    cos_twist, sin_twist = phase_table(fft_outer, fft_inner, FINE)
    second_real = first_real * cos_twist + first_imag * sin_twist
    second_imag = first_imag * cos_twist - first_real * sin_twist
    cos_inner, sin_inner = phase_table(fft_inner, fft_inner, fft_inner)
    third_real = jnp.einsum(
        "qm,iskm->isqk", cos_inner, second_real, precision=TRANSFORM_PRECISION
    ) + jnp.einsum("qm,iskm->isqk", sin_inner, second_imag, precision=TRANSFORM_PRECISION)
    third_imag = jnp.einsum(
        "qm,iskm->isqk", cos_inner, second_imag, precision=TRANSFORM_PRECISION
    ) - jnp.einsum("qm,iskm->isqk", sin_inner, second_real, precision=TRANSFORM_PRECISION)
    factor = station_flags.astype(jnp.float32)[:, None, None] / math.sqrt(FINE)
    stacked = (
        jnp.stack(
            [
                third_real.reshape(inputs_dev, spec_dev, FINE),
                third_imag.reshape(inputs_dev, spec_dev, FINE),
            ]
        )
        * factor
    )
    return stacked.astype(jnp.bfloat16)


def beam_terms(delay_rows, incoming, fine_global):
    phase_turns = delay_rows[:, :, None] * fine_global[None, None, :] % FINE
    angles = phase_turns.astype(jnp.float32) * (2.0 * math.pi / FINE)
    weights = jnp.stack([jnp.cos(angles), jnp.sin(angles)]).astype(jnp.bfloat16)
    products = jnp.einsum("pbik,qitk->pqbtk", weights, incoming, preferred_element_type=jnp.float32)
    volt_real = products[0, 0] + products[1, 1]
    volt_imag = products[0, 1] - products[1, 0]
    return jnp.stack([volt_real, volt_imag])


def cross_products(left_data, right_data, local_count, sub_len):
    row_count = left_data.shape[1]
    col_count = right_data.shape[1]
    spec_count = left_data.shape[2]
    left_rows = left_data.reshape(2 * row_count, spec_count, local_count, sub_len)
    right_rows = right_data.reshape(2 * col_count, spec_count, local_count, sub_len)
    products = jnp.einsum(
        "atlg,btlg->lab", left_rows, right_rows, preferred_element_type=jnp.float32
    )
    vis_real = products[:, :row_count, :col_count] + products[:, row_count:, col_count:]
    vis_imag = products[:, row_count:, :col_count] - products[:, :row_count, col_count:]
    return jnp.stack([vis_real, vis_imag], axis=1)


def on_device(samples, filter_taps, station_flags, channel_keep, beam_delay):
    spectra = fine_spectra(samples, filter_taps, station_flags)
    turned = lax.all_to_all(spectra, "tm", split_axis=3, concat_axis=2, tiled=True)
    inputs_dev = turned.shape[1]
    spectra_all = turned.shape[2]
    fine_dev = turned.shape[3]
    group_len = FINE // OUTCH
    sub_len = min(group_len, fine_dev)
    local_count = fine_dev // sub_len
    tm_index = lax.axis_index("tm")
    stn_index = lax.axis_index("stn")
    fine_start = tm_index * fine_dev
    keep_local = lax.dynamic_slice_in_dim(channel_keep, fine_start, fine_dev, 0)
    keep_wide = keep_local.astype(jnp.bfloat16)
    fine_global = fine_start + jnp.arange(fine_dev, dtype=jnp.int32)
    masked = turned * keep_wide
    vis_local = cross_products(
        masked, lax.all_gather(turned, "stn", axis=1, tiled=True), local_count, sub_len
    )
    own_delays = lax.dynamic_slice_in_dim(beam_delay, stn_index * inputs_dev, inputs_dev, 1)
    voltages = lax.psum_scatter(
        beam_terms(own_delays, turned, fine_global).astype(jnp.bfloat16),
        "stn",
        scatter_dimension=1,
        tiled=True,
    ).astype(jnp.float32)
    beam_energy = jnp.sum(voltages[0] * voltages[0] + voltages[1] * voltages[1], axis=1)
    beam_power = beam_energy * keep_local.astype(jnp.float32) / (INPUTS * spectra_all)
    counts = jnp.sum(channel_keep.reshape(OUTCH, group_len), axis=1)
    first_channel = fine_start // group_len
    local_counts = lax.dynamic_slice_in_dim(counts, first_channel, local_count, 0)
    inv_scale = 1.0 / (local_counts.astype(jnp.float32) * spectra_all)
    scaled = vis_local * inv_scale[:, None, None, None]
    placed = lax.dynamic_update_slice_in_dim(
        jnp.zeros((OUTCH, 2, scaled.shape[2], INPUTS), jnp.float32), scaled, first_channel, 0
    )
    visibilities = lax.psum_scatter(
        placed.astype(jnp.bfloat16), "tm", scatter_dimension=3, tiled=True
    ).astype(jnp.float32)
    return (visibilities, beam_power)


def solution(mesh):
    return jax.shard_map(
        on_device,
        mesh=mesh,
        in_specs=(P(None, "stn", "tm", None), P(), P("stn"), P(), P()),
        out_specs=(P(None, None, "stn", "tm"), P("stn", "tm")),
        check_vma=False,
    )
```

profile of v0, /device:TPU:0, one launch (start us, length us, event | category | flops | bytes accessed | tf_op | source)
XLA Modules:
  0.0 849.8 jit_solution(14004677124410322033)
XLA Ops:
  7.3 28.2 %copy.75 = bf16[2,256,1,20736]{1,3,0,2:T(8,128)(2,1)} copy(bf16[2,256,1,20736]{3,1,2,0:T(8,128)(2,1)} %param.5) | data formatting | bytes 42467328 | tf_op args[0]
  35.5 17.1 %fusion = f32[2,256,3456]{1,2,0:T(8,128)} fusion(bf16[2,256,1,6,3456]{1,4,3,0,2:T(8,128)(2,1)} %bitcast.109, f32[6,3456]{1,0:T(8,128)S(1)} %copy-done.8), kind=kLoop, calls=%fused_computation.1 | loop fusion | flops 30081024 | bytes 28394496 | tf_op jit(solution)/shard_map/reduce_sum | solution.py:25
  52.6 6.4 fusion.122
  59.1 5.4 copy.77
  64.5 6.1 fusion.63
  70.6 5.6 copy.76
  76.3 4.4 fusion.65
  80.8 0.3 copy-done.6
  81.0 2.3 convolution_subtract_fusion
  83.3 3.5 fusion.11
  86.8 3.7 fusion.18
  90.5 5.6 fusion.16
  96.1 3.8 add_bitcast_fusion
  99.8 5.5 copy.82
  105.3 9.3 %copy.86 = f32[1,256,1,3456]{3,1,2,0:T(8,128)} copy(f32[1,256,1,3456]{1,0,3,2:T(1,128)} %bitcast.115) | data formatting | bytes 7077888 | tf_op jit(solution)/shard_map/stack | solution.py:48
  114.6 6.9 subtract_bitcast_fusion
  121.5 5.4 copy.85
  126.9 8.9 %copy.87 = f32[1,256,1,3456]{3,1,2,0:T(8,128)} copy(f32[1,256,1,3456]{1,0,3,2:T(1,128)} %bitcast.116) | data formatting | bytes 7077888 | tf_op jit(solution)/shard_map/stack | solution.py:48
  135.8 5.4 fusion.9
  141.3 9.8 %copy.88 = bf16[2,256,1,3456]{1,0,2,3:T(2,128)(2,1)} copy(bf16[2,256,1,3456]{3,1,2,0:T(8,128)(2,1)} %fusion.9) | data formatting | bytes 7077888 | tf_op jit(solution)/shard_map/convert_element_type | solution.py:56
  151.1 86.8 %all_to_all.15 = bf16[2,256,1,3456]{1,0,2,3:T(2,128)(2,1)S(1)} all-to-all(bf16[2,256,1,3456]{1,0,2,3:T(2,128)(2,1)} %copy.88), channel_id=1, replica_groups=mesh['stn'=4,'tm'=8] {'tm'}, dimensions={3} | all-to-all | bytes 7077888 | tf_op jit(solution)/shard_map/all_to_all | solution.py:85
  237.8 1.8 copy-done.4
  239.6 2.3 copy.89
  242.2 0.1 reduce_sum.28
  242.4 122.2 %cosine_convert_fusion = (bf16[1,64,256,432]{2,1,0,3:T(8,128)(2,1)}, bf16[1,64,256,432]{2,1,0,3:T(8,128)(2,1)}) fusion(s32[432]{0:T(512)S(1)} %iota_add_fusion, s32[64,256]{1,0:T(8,128)S(1)} %constant_dynamic-slice_fusion), kind=kLoop, calls=%fused_computation.10 | loop fusion | flops 77856768 | bytes 28378816 | tf_op jit(solution)/shard_map/convert.5
  364.7 27.3 %fusion.24 = f32[2,2,64,8,432]{2,3,0,1,4:T(8,128)} fusion(bf16[1,64,256,432]{2,1,0,3:T(8,128)(2,1)} %get-tuple-element.15, bf16[1,64,256,432]{2,1,0,3:T(8,128)(2,1)} %get-tuple-element.14, bf16[2,256,8,432,1]{1,3,2,0,4:T(8,128)(2,1)S(1)} %bitcast.114), kind=kOutput, calls=%fused_computation.40 | convolution fusion | flops 509607936 | bytes 35389440 | tf_op jit(solution)/shard_map/pbik,qitk->pqbtk/dot_general | solution.py:63
  392.0 2.2 fusion.37
  394.2 2.2 fusion.38
  396.4 0.4 pad_maximum_fusion
  396.8 3.1 copy.95
  400.0 9.2 %all_to_all.12 = bf16[512,8,2,216]{0,3,2,1:T(8,128)(2,1)} reshape(bf16[2,256,1,3456]{1,0,2,3:T(2,128)(2,1)} %copy-done.4) | data formatting | bytes 7077888 | tf_op jit(solution)/shard_map/all_to_all | solution.py:85
  409.2 26.5 %copy.90 = bf16[2,1024,8,432]{1,0,3,2:T(2,128)(2,1)} copy(bf16[2,1024,8,432]{1,3,2,0:T(8,128)(2,1)} %all-gather.2.cloned.1.call-done) | data formatting | bytes 28311552 | tf_op jit(solution)/shard_map/all_gather | solution.py:100
  435.7 23.7 %reshape.240 = bf16[2048,8,2,216]{0,3,2,1:T(8,128)(2,1)} reshape(bf16[2,1024,8,432]{1,0,3,2:T(2,128)(2,1)} %copy.90) | data formatting | bytes 28311552 | tf_op jit(solution)/shard_map/reshape | solution.py:74
  459.4 12.3 %convolution_bitcast_fusion = f32[2,512,2048]{2,1,0:T(8,128)S(1)} fusion(bf16[2048,8,2,216]{0,3,2,1:T(8,128)(2,1)} %reshape.240, bf16[512,8,2,216]{0,3,2,1:T(8,128)(2,1)} %all_to_all.12, bf16[2,216]{1,0:T(2,128)(2,1)S(1)} %mul.249), kind=kOutput, calls=%fused_computation.17 | convolution fusion | flops 7249526784 | bytes 26084192 | tf_op jit(solution)/shard_map/atlg,btlg->lab/dot_general | solution.py:75
  471.7 1.0 fusion.28
  472.7 6.0 broadcast_in_dim.2
  478.7 2.0 copy_dynamic-update-slice_fusion
  480.7 41.2 %copy.102 = bf16[16,2,256,1024]{2,1,0,3:T(2,128)(2,1)} copy(bf16[16,2,256,1024]{3,2,1,0:T(8,128)(2,1)} %copy_dynamic-update-slice_fusion) | data formatting | bytes 33554432
  521.9 27.6 %reshape.250 = bf16[1024,8192]{1,0:T(8,128)(2,1)} reshape(bf16[1024,16,2,256]{3,2,1,0:T(2,128)(2,1)} %bitcast.110) | data formatting | bytes 33554432
  549.6 1.0 convert_element_type.111
  550.6 0.1 fusion.40
  550.7 0.1 copy.104
  550.8 0.1 multiply_multiply_fusion
  551.0 0.7 copy.97
  551.7 279.4 %reduce-scatter.7.cloned.1.call-done = bf16[128,8192]{1,0:T(8,128)(2,1)} async-done(((bf16[1024,8192]{1,0:T(8,128)(2,1)}), bf16[128,8192]{1,0:T(8,128)(2,1)}) %reduce-scatter.7.cloned.1.call-update) | async-done | bytes 2097168
  831.0 4.5 reshape.251
  835.5 5.0 copy.103
  840.5 2.5 convert_element_type.109
  (36 shorter events, 0.7 us)
Async XLA Ops:
  7.2 235.3 %copy-start = (s32[64,1024]{1,0:T(8,128)S(1)}, s32[64,1024]{1,0:T(8,128)}, u32[]{:S(2)}) copy-start(s32[64,1024]{1,0:T(8,128)} %param.9) | copy-start | bytes 786436
  7.2 402.0 %all-gather.2.cloned.1.call-start = ((), (), s32[]{:S(2)}) async-start(), calls=%async_computation.3 | async-start | bytes 17694720 | tf_op jit(solution)/shard_map/all_gather | solution.py:100
  7.3 28.2 %copy-start.8 = (f32[6,3456]{1,0:T(8,128)S(1)}, f32[6,3456]{1,0:T(8,128)}, u32[]{:S(2)}) copy-start(f32[6,3456]{1,0:T(8,128)} %param.6) | copy-start | bytes 248836
  76.3 4.5 copy-start.3
  76.3 4.7 copy-start.6
  81.0 2.3 copy-start.2
  86.8 9.3 %copy-start.5 = (f32[256,27,128]{2,1,0:T(8,128)}, f32[256,27,128]{2,1,0:T(8,128)S(1)}, u32[]{:S(2)}) copy-start(f32[256,27,128]{2,1,0:T(8,128)S(1)} %get-tuple-element.8) | copy-start | bytes 10616836
  126.9 8.9 %copy-start.10 = (s32[256]{0:T(256)S(1)}, s32[256]{0:T(256)}, u32[]{:S(2)}) copy-start(s32[256]{0:T(256)} %param.7) | copy-start | bytes 3076
  237.8 1.8 copy-start.4
  239.6 2.4 copy-start.9
  241.9 307.7 %reduce-scatter.5.cloned.1.call-start = ((), (), s32[]{:S(2)}) async-start(), calls=%async_computation.4 | async-start | bytes 1310720 | tf_op jit(solution)/shard_map/reduce_scatter | solution.py:103
  242.4 122.2 %copy-start.7 = (bf16[2,256,1,3456]{1,3,0,2:T(8,128)(2,1)S(1)}, bf16[2,256,1,3456]{1,3,0,2:T(8,128)(2,1)}, u32[]{:S(2)}) copy-start(bf16[2,256,1,3456]{1,3,0,2:T(8,128)(2,1)} %copy.89) | copy-start | bytes 10616836
  400.0 431.1 %reduce-scatter.7.cloned.1.call-start = ((), (), s32[]{:S(2)}) async-start(), calls=%async_computation.5 | async-start | bytes 18874368
  835.5 7.5 copy-start.1
Sparse Core Ops, SparseCore 0:
  242.0 91.5 all-gather.1
  400.1 23.5 reduce-scatter.4
  549.7 281.3 reduce-scatter.6
where the time goes:
time: 858 us; the launch traced here: 850 us
  waiting for transfers between devices  279 us (33%)
  local copies, waits for them, and re-layouts  237 us (28%)
  other arithmetic  157 us (18%)
  blocking collectives  86.8 us (10%)
  matrix products  75.8 us (9%)
  between operations  14.2 us (2%)
    unnamed x4, waiting for transfers between devices  279 us
    another operation x1, other arithmetic  122 us
    unnamed x29, local copies, waits for them, and re-layouts  109 us
    all_to_all x1, blocking collectives, on_device(): lax.all_to_all(spectra, 'tm', split_axis=3, concat_axis=2, tiled=True)  86.8 us
    dot_general x1, matrix products, beam_terms(): jnp.einsum('pbik,qitk->pqbtk', weights, incoming, preferred_element_type=...  27.3 us
    all_gather x1, local copies, waits for them, and re-layouts, on_device(): lax.all_gather(turned, 'stn', axis=1, tiled=True)  26.5 us
    reshape x1, local copies, waits for them, and re-layouts, cross_products(): right_data.reshape(2 * col_count, spec_count, local_count, sub_len)  23.7 us
    another operation x2, local copies, waits for them, and re-layouts, fine_spectra(): jnp.stack([third_real.reshape(inputs_dev, spec_dev, FINE), third_imag.res...  18.2 us
  transfers between devices with their start and end apart: 3, of which 1 were waited for; matrix products, arithmetic and copies ran while one was open for 35% of the time, Pallas kernels for 0%

commit v1 on v0

--- a/solution.py
+++ b/solution.py
@@ -1,3 +1,4 @@
+import functools
 import math
 import jax
 import jax.numpy as jnp
@@ -9,6 +10,36 @@
 OUTCH = 16
 TAPS = 6
 TRANSFORM_PRECISION = lax.Precision.HIGH
+
+
+def pair_the_levels_all(z_in, dimension_no):
+    z_in = jnp.moveaxis(z_in, 0, dimension_no)
+    e_next = z_in.shape
+    return z_in.reshape(
+        *e_next[:dimension_no],
+        e_next[dimension_no] * e_next[dimension_no + 1],
+        *e_next[dimension_no + 2 :]
+    )
+
+
+def move_waves(x_part, group_axis):
+    reply, val2 = (lax.axis_size(group_axis), lax.axis_index(group_axis))
+    v1, next_value = (x_part[None], 1)
+    while next_value < reply:
+        found_now = lax.ppermute(
+            v1, group_axis, list(map(lambda tick: (tick, tick ^ next_value), range(reply)))
+        )
+        clean = val2 & next_value == 0
+        v1 = jnp.concatenate([jnp.where(clean, v1, found_now), jnp.where(clean, found_now, v1)])
+        next_value *= 2
+    return v1
+
+
+def arrange_ways(packet, array_axis, mat):
+    return pair_the_levels_all(move_waves(packet, mat), array_axis)
+
+
+fill_works = functools.partial(arrange_ways, array_axis=1, mat="stn")
 
 
 def phase_table(row_count, col_count, modulus):
@@ -96,9 +127,7 @@
     keep_wide = keep_local.astype(jnp.bfloat16)
     fine_global = fine_start + jnp.arange(fine_dev, dtype=jnp.int32)
     masked = turned * keep_wide
-    vis_local = cross_products(
-        masked, lax.all_gather(turned, "stn", axis=1, tiled=True), local_count, sub_len
-    )
+    vis_local = cross_products(masked, fill_works(turned), local_count, sub_len)
     own_delays = lax.dynamic_slice_in_dim(beam_delay, stn_index * inputs_dev, inputs_dev, 1)
     voltages = lax.psum_scatter(
         beam_terms(own_delays, turned, fine_global).astype(jnp.bfloat16),

time: 858 us -> 890 us (1.037)
  other arithmetic: 157 us -> 172 us
  local copies, waits for them, and re-layouts: 237 us -> 246 us
    transpose x0 -> x1, local copies, waits for them, and re-layouts: none -> 34.1 us  [pair_the_levels_all(): z_in = jnp.moveaxis(z_in, 0, dimension_no)]
    all_gather x1 -> x0, local copies, waits for them, and re-layouts: 26.5 us -> none  [on_device(): lax.all_gather(turned, 'stn', axis=1, tiled=True)]
    reshape x1 -> x0, local copies, waits for them, and re-layouts: 23.7 us -> none  [cross_products(): right_data.reshape(2 * col_count, spec_count, local_count, sub_len)]
    another operation x2 -> x3, local copies, waits for them, and re-layouts: 11.1 us -> 34.7 us  [the longest x1 23.6 us: cross_products(): right_data.reshape(2 * col_count, spec_count, local_count, sub_len)]
    select_n x0 -> x2, other arithmetic: none -> 9.37 us  [move_waves(): jnp.where(clean, v1, found_now)]
    unnamed x29 -> x33, local copies, waits for them, and re-layouts: 109 us -> 111 us
    unnamed x4 -> x3, waiting for transfers between devices: 279 us -> 278 us
  transfers between devices with their start and end apart: 3 -> 4, of which waited for: 1 -> 2; matrix products, arithmetic and copies ran while one was open for 35% -> 36% of each run, Pallas kernels for 0% -> 0%
where the time goes in v1:
time: 890 us; the launch traced here: 881 us
  waiting for transfers between devices  285 us (32%)
  local copies, waits for them, and re-layouts  246 us (28%)
  other arithmetic  172 us (19%)
  blocking collectives  86.9 us (10%)
  matrix products  75.7 us (9%)
  between operations  14.6 us (2%)
    unnamed x3, waiting for transfers between devices  278 us
    another operation x1, other arithmetic  122 us
    unnamed x33, local copies, waits for them, and re-layouts  111 us
    all_to_all x1, blocking collectives, on_device(): lax.all_to_all(spectra, 'tm', split_axis=3, concat_axis=2, tiled=True)  86.9 us
    transpose x1, local copies, waits for them, and re-layouts, pair_the_levels_all(): z_in = jnp.moveaxis(z_in, 0, dimension_no)  34.1 us
    dot_general x1, matrix products, beam_terms(): jnp.einsum('pbik,qitk->pqbtk', weights, incoming, preferred_element_type=...  27.3 us
    another operation x1, local copies, waits for them, and re-layouts, cross_products(): right_data.reshape(2 * col_count, spec_count, local_count, sub_len)  23.6 us
    another operation x2, local copies, waits for them, and re-layouts, fine_spectra(): jnp.stack([third_real.reshape(inputs_dev, spec_dev, FINE), third_imag.res...  18.2 us
  transfers between devices with their start and end apart: 4, of which 2 were waited for; matrix products, arithmetic and copies ran while one was open for 36% of the time, Pallas kernels for 0%

profile of v1, /device:TPU:0, one launch (start us, length us, event | category | flops | bytes accessed | tf_op | source)
XLA Modules:
  0.0 881.1 jit_solution(2485124374473169535)
XLA Ops:
  7.3 28.3 %copy.78 = bf16[2,256,1,20736]{1,3,0,2:T(8,128)(2,1)} copy(bf16[2,256,1,20736]{3,1,2,0:T(8,128)(2,1)} %param.5) | data formatting | bytes 42467328 | tf_op args[0]
  35.6 17.1 %fusion = f32[2,256,3456]{1,2,0:T(8,128)} fusion(bf16[2,256,1,6,3456]{1,4,3,0,2:T(8,128)(2,1)} %bitcast.112, f32[6,3456]{1,0:T(8,128)S(1)} %copy-done.10), kind=kLoop, calls=%fused_computation.1 | loop fusion | flops 30081024 | bytes 28394496 | tf_op jit(solution)/shard_map/reduce_sum | solution.py:56
  52.8 6.4 fusion.122
  59.2 5.4 copy.80
  64.6 6.1 fusion.63
  70.7 5.7 copy.79
  76.4 4.4 fusion.65
  81.2 2.3 convolution_subtract_fusion
  83.5 3.5 fusion.11
  87.0 3.7 fusion.18
  90.6 5.6 fusion.16
  96.2 3.8 add_bitcast_fusion
  100.0 5.5 copy.85
  105.5 9.3 %copy.89 = f32[1,256,1,3456]{3,1,2,0:T(8,128)} copy(f32[1,256,1,3456]{1,0,3,2:T(1,128)} %bitcast.117) | data formatting | bytes 7077888 | tf_op jit(solution)/shard_map/stack | solution.py:79
  114.8 6.9 subtract_bitcast_fusion
  121.7 5.4 copy.88
  127.1 8.9 %copy.90 = f32[1,256,1,3456]{3,1,2,0:T(8,128)} copy(f32[1,256,1,3456]{1,0,3,2:T(1,128)} %bitcast.118) | data formatting | bytes 7077888 | tf_op jit(solution)/shard_map/stack | solution.py:79
  136.0 5.4 fusion.9
  141.5 9.8 %copy.91 = bf16[2,256,1,3456]{1,0,2,3:T(2,128)(2,1)} copy(bf16[2,256,1,3456]{3,1,2,0:T(8,128)(2,1)} %fusion.9) | data formatting | bytes 7077888 | tf_op jit(solution)/shard_map/convert_element_type | solution.py:87
  151.2 86.9 %all_to_all.15 = bf16[2,256,1,3456]{1,0,2,3:T(2,128)(2,1)S(1)} all-to-all(bf16[2,256,1,3456]{1,0,2,3:T(2,128)(2,1)} %copy.91), channel_id=1, replica_groups=mesh['stn'=4,'tm'=8] {'tm'}, dimensions={3} | all-to-all | bytes 7077888 | tf_op jit(solution)/shard_map/all_to_all | solution.py:116
  238.2 1.8 copy-done.4
  239.9 2.3 copy.92
  242.2 6.6 collective-permute-done
  248.7 3.5 broadcast_select_fusion.3
  252.3 3.9 pad_maximum_fusion
  256.3 1.1 copy-done.7
  257.4 1.5 collective-permute-start.1
  259.4 122.0 %cosine_convert_fusion = (bf16[1,64,256,432]{2,1,0,3:T(8,128)(2,1)}, bf16[1,64,256,432]{2,1,0,3:T(8,128)(2,1)}) fusion(s32[432]{0:T(512)S(1)} %iota_add_fusion, s32[64,256]{1,0:T(8,128)S(1)} %constant_dynamic-slice_fusion), kind=kLoop, calls=%fused_computation.10 | loop fusion | flops 77856768 | bytes 28378816 | tf_op jit(solution)/shard_map/convert.5
  381.4 27.3 %fusion.24 = f32[2,2,64,8,432]{2,3,0,1,4:T(8,128)} fusion(bf16[1,64,256,432]{2,1,0,3:T(8,128)(2,1)} %get-tuple-element.19, bf16[1,64,256,432]{2,1,0,3:T(8,128)(2,1)} %get-tuple-element.18, bf16[2,256,8,432,1]{1,0,3,2,4:T(2,128)(2,1)S(1)} %bitcast.114), kind=kOutput, calls=%fused_computation.46 | convolution fusion | flops 509607936 | bytes 35389440 | tf_op jit(solution)/shard_map/pbik,qitk->pqbtk/dot_general | solution.py:94
  408.7 2.2 fusion.37
  410.9 2.2 fusion.38
  413.5 3.1 copy.99
  416.7 9.2 %all_to_all.12 = bf16[512,8,2,216]{0,3,2,1:T(8,128)(2,1)} reshape(bf16[2,256,1,3456]{1,0,2,3:T(2,128)(2,1)} %copy-done.4) | data formatting | bytes 7077888 | tf_op jit(solution)/shard_map/all_to_all | solution.py:116
  425.9 5.8 broadcast_select_fusion.1
  431.7 2.0 maximum_bitcast_fusion.2
  433.7 34.1 %copy.93 = bf16[2,4,256,8,432]{2,1,0,4,3:T(4,128)(2,1)} copy(bf16[2,4,256,8,432]{2,4,3,0,1:T(8,128)(2,1)S(1)} %maximum_bitcast_fusion.2) | data formatting | bytes 28311552 | tf_op jit(solution)/shard_map/transpose | solution.py:16
  467.8 23.6 %reshape_reshape.3 = bf16[2048,8,2,216]{0,3,2,1:T(8,128)(2,1)} reshape(bf16[2,4,256,8,432]{2,1,0,4,3:T(4,128)(2,1)} %copy.93) | data formatting | bytes 28311552 | tf_op jit(solution)/shard_map/reshape;reshape | solution.py:105
  491.3 12.3 %convolution_bitcast_fusion = f32[2,512,2048]{2,1,0:T(8,128)S(1)} fusion(bf16[2048,8,2,216]{0,3,2,1:T(8,128)(2,1)} %reshape_reshape.3, bf16[512,8,2,216]{0,3,2,1:T(8,128)(2,1)} %all_to_all.12, bf16[2,216]{1,0:T(2,128)(2,1)S(1)} %mul.249), kind=kOutput, calls=%fused_computation.21 | convolution fusion | flops 7249526784 | bytes 26084192 | tf_op jit(solution)/shard_map/atlg,btlg->lab/dot_general | solution.py:106
  503.6 1.0 fusion.28
  504.6 6.0 broadcast_in_dim.4
  510.6 2.0 copy_dynamic-update-slice_fusion
  512.6 41.3 %copy.108 = bf16[16,2,256,1024]{2,1,0,3:T(2,128)(2,1)} copy(bf16[16,2,256,1024]{3,2,1,0:T(8,128)(2,1)} %copy_dynamic-update-slice_fusion) | data formatting | bytes 33554432
  553.9 27.7 %reshape.247 = bf16[1024,8192]{1,0:T(8,128)(2,1)} reshape(bf16[1024,16,2,256]{3,2,1,0:T(2,128)(2,1)} %bitcast.113) | data formatting | bytes 33554432
  581.6 1.0 convert_element_type.111
  583.7 278.3 %reduce-scatter.7.cloned.1.call-done = bf16[128,8192]{1,0:T(8,128)(2,1)} async-done(((bf16[1024,8192]{1,0:T(8,128)(2,1)}), bf16[128,8192]{1,0:T(8,128)(2,1)}) %reduce-scatter.7.cloned.1.call-update) | async-done | bytes 2097168
  862.1 4.5 reshape.248
  866.5 5.0 copy.109
  871.5 2.5 convert_element_type.109
  (45 shorter events, 2.5 us)
Async XLA Ops:
  7.2 252.2 %copy-start = (s32[64,1024]{1,0:T(8,128)S(1)}, s32[64,1024]{1,0:T(8,128)}, u32[]{:S(2)}) copy-start(s32[64,1024]{1,0:T(8,128)} %param.9) | copy-start | bytes 786436
  7.2 574.4 %reduce-scatter.5.cloned.1.call-start = ((), (), s32[]{:S(2)}) async-start(), calls=%async_computation.3 | async-start | bytes 1310720 | tf_op jit(solution)/shard_map/reduce_scatter | solution.py:132
  7.3 28.3 %copy-start.10 = (f32[6,3456]{1,0:T(8,128)S(1)}, f32[6,3456]{1,0:T(8,128)}, u32[]{:S(2)}) copy-start(f32[6,3456]{1,0:T(8,128)} %param.6) | copy-start | bytes 248836
  76.4 4.5 copy-start.3
  76.4 4.7 copy-start.9
  81.2 2.3 copy-start.2
  87.0 9.3 %copy-start.8 = (f32[256,27,128]{2,1,0:T(8,128)}, f32[256,27,128]{2,1,0:T(8,128)S(1)}, u32[]{:S(2)}) copy-start(f32[256,27,128]{2,1,0:T(8,128)S(1)} %get-tuple-element.10) | copy-start | bytes 10616836
  127.1 8.9 %copy-start.12 = (s32[256]{0:T(256)S(1)}, s32[256]{0:T(256)}, u32[]{:S(2)}) copy-start(s32[256]{0:T(256)} %param.7) | copy-start | bytes 3076
  238.2 1.8 copy-start.4
  242.2 6.6 collective-permute-start
  252.3 4.0 copy-start.6
  252.3 5.1 copy-start.7
  252.3 6.6 copy-start.11
  257.4 168.5 %collective-permute-start.1 = (bf16[2,2,256,8,432]{2,4,3,1,0:T(8,128)(2,1)}, bf16[2,2,256,8,432]{2,4,3,1,0:T(8,128)(2,1)}, u32[]{:S(2)}, u32[]{:S(2)}) collective-permute-start(bf16[2,2,256,8,432]{2,4,3,1,0:T(8,128)(2,1)} %pad_maximum_fusion), channel_id=1, source_target_pairs={{0,16},{8,24},{16,0},{24,8},{1,17},{9,25},{17,1},{25,9},{2,18},{10... | collective-permute-start | bytes 21233672 | tf_op jit(solution)/shard_map/ppermute | solution.py:29
  259.4 122.1 %copy-start.5 = (bf16[2,256,1,3456]{1,0,2,3:T(2,128)(2,1)S(1)}, bf16[2,256,1,3456]{1,0,2,3:T(2,128)(2,1)}, u32[]{:S(2)}) copy-start(bf16[2,256,1,3456]{1,0,2,3:T(2,128)(2,1)} %copy-done.4) | copy-start | bytes 10616836
  416.7 445.4 %reduce-scatter.7.cloned.1.call-start = ((), (), s32[]{:S(2)}) async-start(), calls=%async_computation.4 | async-start | bytes 18874368
  866.5 7.5 copy-start.1
Sparse Core Ops, SparseCore 0:
  416.8 22.5 reduce-scatter.4
  581.7 280.2 reduce-scatter.6
